TPU v7x, 256 devices: a whole 4x4x8 slice. The times are simulated.
256 devices in a mesh: row: 16 (over y, z_lo), col: 16 (over x, z_hi, core).
Axes of the slice: x: 4, y: 4, z: 8 (z_hi: 2, z_lo: 4; z = z_hi * 4 + z_lo), core: 2. Of those that a mesh axis runs over, the one named last changes fastest.
Arguments:
- momentum: bfloat16 [5376, 10240], P('row', 'col'), may hold values from -6 to 6
Outputs:
- update: bfloat16 [5376, 10240], P('row', 'col')
All inputs are finite; a program needn't handle non-finite values.
Results may differ from a plain program's by a relative error of at most 0.0059.
Values may be sent and summed in bfloat16 or wider, within the bound.
No kernel may reach another device: no remote copies, remote signals or barrier semaphores. Data moves between devices by JAX's collectives and lax.ppermute only.
A program may use at most 64 MiB of HBM per device.

v0:
```python
import jax
import jax.numpy as jnp
from jax import lax
from jax.sharding import PartitionSpec as P

C = 10240


coef_a = 3.4445
coef_b = -4.775
coef_c = 2.0315


def body(momentum):
    full_cols = lax.all_gather(momentum, "row", axis=0, tiled=True)
    raw_block = lax.psum_scatter(
        jnp.dot(full_cols, momentum.T, preferred_element_type=jnp.float32),
        "col",
        scatter_dimension=0,
        tiled=True,
    ).T
    gram_block = (raw_block / C).astype(jnp.bfloat16)
    gram_rows = lax.all_gather(gram_block, "col", axis=1, tiled=True)
    squared = jnp.dot(
        gram_rows,
        lax.all_gather(gram_block, "row", axis=0, tiled=True),
        preferred_element_type=jnp.float32,
    )
    poly = (coef_b * gram_block.astype(jnp.float32) + coef_c * squared).astype(jnp.bfloat16)
    product = jnp.dot(
        lax.all_gather(poly, "col", axis=1, tiled=True),
        full_cols,
        preferred_element_type=jnp.float32,
    )
    return (coef_a * momentum.astype(jnp.float32) + product).astype(jnp.bfloat16)


def solution(mesh):
    return jax.shard_map(
        body,
        mesh=mesh,
        in_specs=(P("row", "col"),),
        out_specs=P("row", "col"),
        check_vma=False,
    )
```

profile of v0, /device:TPU:1, one launch (start us, length us, event | category | flops | bytes accessed | tf_op | source)
XLA Modules:
  0.0 587.7 jit_solution(4288785313415987661)
XLA Ops:
  6.5 0.0 all-gather.5.cloned.1.call-start
  6.5 0.7 all-gather.5.cloned.1.call-update
  7.3 0.0 reduce-scatter.2.cloned.1.call-start
  7.3 161.0 %all-gather.5.cloned.1.call-done = bf16[5376,640]{1,0:T(8,128)(2,1)} async-done(((bf16[336,640]{1,0:T(8,128)(2,1)}), bf16[5376,640]{1,0:T(8,128)(2,1)}) %all-gather.5.cloned.1.call-update) | async-done | bytes 6881296 | tf_op jit(solution)/shard_map/all_gather | solution.py:15
  168.3 10.3 %fusion.4 = f32[5376,336]{1,0:T(8,128)} fusion(bf16[5376,640]{1,0:T(8,128)(2,1)} %all-gather.5.cloned.1.call-done, bf16[336,640]{1,0:T(8,128)(2,1)} %param.1), kind=kOutput, calls=%fused_computation.7 | convolution fusion | flops 2312110080 | bytes 14536704 | tf_op jit(solution)/shard_map/dot_general | solution.py:17
  178.6 0.0 reduce-scatter.2.cloned.1.call-update
  178.6 0.0 all-gather.7.cloned.1.call-start
  178.7 139.0 %reduce-scatter.2.cloned.1.call-done = f32[336,336]{1,0:T(8,128)} async-done(((f32[5376,336]{1,0:T(8,128)}), f32[336,336]{1,0:T(8,128)}) %reduce-scatter.2.cloned.1.call-update) | async-done | bytes 451600 | tf_op jit(solution)/shard_map/reduce_scatter | solution.py:16
  317.6 1.8 fusion.3
  319.4 0.0 all-gather.7.cloned.1.call-update
  319.4 0.0 all-gather.9.cloned.1.call-start
  319.5 1.8 copy.2
  321.3 0.0 all-gather.9.cloned.1.call-update
  321.3 0.0 copy-start
  321.3 0.0 all-gather.11.cloned.1.call-start
  321.4 73.3 %all-gather.7.cloned.1.call-done = bf16[336,5376]{0,1:T(8,128)(2,1)} async-done(((bf16[336,336]{0,1:T(8,128)(2,1)}), bf16[336,5376]{0,1:T(8,128)(2,1)}) %all-gather.7.cloned.1.call-update) | async-done | bytes 3612688 | tf_op jit(solution)/shard_map/all_gather | solution.py:23
  394.7 97.5 %all-gather.9.cloned.1.call-done = bf16[5376,336]{1,0:T(8,128)(2,1)} async-done(((bf16[336,336]{1,0:T(8,128)(2,1)}), bf16[5376,336]{1,0:T(8,128)(2,1)}) %all-gather.9.cloned.1.call-update) | async-done | bytes 3612688 | tf_op jit(solution)/shard_map/all_gather | solution.py:26
  492.1 6.2 %fusion.2 = bf16[336,336]{0,1:T(8,128)(2,1)} fusion(bf16[336,5376]{0,1:T(8,128)(2,1)} %all-gather.7.cloned.1.call-done, bf16[5376,336]{1,0:T(8,128)(2,1)} %all-gather.9.cloned.1.call-done, bf16[336,336]{0,1:T(8,128)(2,1)} %fusion.3), kind=kOutput, calls=%fused_computation.4 | convolution fusion | flops 1214422272 | bytes 7676928 | tf_op jit(solution)/shard_map/dot_general | solution.py:24
  498.4 0.0 all-gather.11.cloned.1.call-update
  498.4 74.8 %all-gather.11.cloned.1.call-done = bf16[336,5376]{0,1:T(8,128)(2,1)} async-done(((bf16[336,336]{0,1:T(8,128)(2,1)}), bf16[336,5376]{0,1:T(8,128)(2,1)}) %all-gather.11.cloned.1.call-update) | async-done | bytes 3612688 | tf_op jit(solution)/shard_map/all_gather | solution.py:31
  573.2 0.0 copy-done
  573.2 8.0 %fusion = bf16[336,640]{1,0:T(8,128)(2,1)} fusion(bf16[336,5376]{0,1:T(8,128)(2,1)} %all-gather.11.cloned.1.call-done, bf16[5376,640]{1,0:T(8,128)(2,1)} %all-gather.5.cloned.1.call-done, bf16[336,640]{1,0:T(8,128)(2,1)S(1)} %copy-done), kind=kOutput, calls=%fused_computation.1 | convolution fusion | flops 2312970240 | bytes 11354112 | tf_op jit(solution)/shard_map/dot_general | solution.py:30
Async XLA Ops:
  6.5 161.8 %all-gather.5.cloned.1.call-start = ((), (), s32[]{:S(2)}) async-start(), calls=%async_computation.1 | async-start | bytes 7311360 | tf_op jit(solution)/shard_map/all_gather | solution.py:15
  7.3 310.4 %reduce-scatter.2.cloned.1.call-start = ((), (), s32[]{:S(2)}) async-start(), calls=%async_computation.2 | async-start | bytes 8773632 | tf_op jit(solution)/shard_map/reduce_scatter | solution.py:16
  178.6 216.1 %all-gather.7.cloned.1.call-start = ((), (), s32[]{:S(2)}) async-start(), calls=%async_computation.3 | async-start | bytes 4386816 | tf_op jit(solution)/shard_map/all_gather | solution.py:23
  319.4 172.7 %all-gather.9.cloned.1.call-start = ((), (), s32[]{:S(2)}) async-start(), calls=%async_computation.4 | async-start | bytes 4386816 | tf_op jit(solution)/shard_map/all_gather | solution.py:26
  321.3 251.9 %copy-start = (bf16[336,640]{1,0:T(8,128)(2,1)S(1)}, bf16[336,640]{1,0:T(8,128)(2,1)}, u32[]{:S(2)}) copy-start(bf16[336,640]{1,0:T(8,128)(2,1)} %param.1) | copy-start | bytes 1290244
  321.3 251.9 %all-gather.11.cloned.1.call-start = ((), (), s32[]{:S(2)}) async-start(), calls=%async_computation.5 | async-start | bytes 4386816 | tf_op jit(solution)/shard_map/all_gather | solution.py:31
Sparse Core Ops, SparseCore 0:
  9.1 159.1 all-gather.4
  178.7 138.8 reduce-scatter.1
  320.6 74.0 all-gather.6
  396.4 95.6 all-gather.8
  498.5 74.6 all-gather.10
where the time goes:
time: 588 us
  waiting for transfers between devices  546 us (93%)
  matrix products  24.5 us (4%)
  between operations  13.1 us (2%)
    all_gather x1, waiting for transfers between devices, body(): full_cols = lax.all_gather(momentum, 'row', axis=0, tiled=True)  161 us
    reduce_scatter x1, waiting for transfers between devices, body(): lax.psum_scatter(jnp.dot(full_cols, momentum.T, preferred_element_type=jn...  139 us
    all_gather x1, waiting for transfers between devices, body(): lax.all_gather(gram_block, 'row', axis=0, tiled=True)  97.5 us
    all_gather x1, waiting for transfers between devices, body(): lax.all_gather(poly, 'col', axis=1, tiled=True)  74.8 us
    all_gather x1, waiting for transfers between devices, body(): gram_rows = lax.all_gather(gram_block, 'col', axis=1, tiled=True)  73.3 us
  transfers between devices with their start and end apart: 5, of which 5 were waited for; matrix products, arithmetic and copies ran while one was open for 0% of the time, Pallas kernels for 0%

commit v1 on v0

v1 whole, which is shorter than its diff:
```python
import jax
import jax.numpy as jnp
from jax import lax
from jax.sharding import Mesh, PartitionSpec as P

C = 10240
B = 336

coef_a = 3.4445
coef_b = -4.775
coef_c = 2.0315

AXES = ("y", "zl", "x", "zh", "core")


def send_xor(v, axis, size, k):
    return lax.ppermute(v, axis, [(i, i ^ k) for i in range(size)])


def send_up(v, axis, size, k):
    return lax.ppermute(v, axis, [(i, (i + k) % size) for i in range(size)])


def gather_z(v):
    return jnp.concatenate([v] + [send_xor(v, "zl", 4, t) for t in (1, 2, 3)], axis=0)


def gather_y(v):
    return jnp.concatenate([v] + [send_up(v, "y", 4, -s) for s in (1, 2, 3)], axis=0)


def reduce_y(partial):
    total = partial[:B]
    sent = partial.astype(jnp.bfloat16)
    for s in (1, 2, 3):
        total = total + send_up(sent[s * B : (s + 1) * B], "y", 4, s).astype(jnp.float32)
    return total


def body(momentum):
    core = lax.axis_index("core")
    xi = lax.axis_index("x")
    half, quarter = 2 * B, B // 2
    x2 = gather_z(momentum)
    x1 = gather_y(momentum)
    partial = lax.dot_general(
        x1, x2, (((1,), (1,)), ((), ())), preferred_element_type=jnp.float32
    )
    kept = lax.dynamic_slice_in_dim(partial, core * half, half, 0)
    given = lax.dynamic_slice_in_dim(partial, (1 - core) * half, half, 0)
    got = send_xor(given.astype(jnp.bfloat16), "core", 2, 1)
    chip = kept + got.astype(jnp.float32)
    chip_sent = chip.astype(jnp.bfloat16)
    total = lax.dynamic_slice_in_dim(chip, xi * quarter, quarter, 0)
    for k in (1, 2, 3):
        piece = lax.dynamic_slice_in_dim(chip_sent, (xi ^ k) * quarter, quarter, 0)
        total = total + send_xor(piece, "x", 4, k).astype(jnp.float32)
    total = total + send_xor(total.astype(jnp.bfloat16), "zh", 2, 1).astype(jnp.float32)
    mine = (total / C).astype(jnp.bfloat16)
    rows = jnp.zeros((half, 4 * B), jnp.bfloat16)
    rows = lax.dynamic_update_slice_in_dim(rows, mine, xi * quarter, 0)
    for k in (1, 2, 3):
        rows = lax.dynamic_update_slice_in_dim(
            rows, send_xor(mine, "x", 4, k), (xi ^ k) * quarter, 0
        )
    other = send_xor(rows, "core", 2, 1)
    gram = jnp.zeros((4 * B, 4 * B), jnp.bfloat16)
    gram = lax.dynamic_update_slice_in_dim(gram, rows, core * half, 0)
    gram = lax.dynamic_update_slice_in_dim(gram, other, (1 - core) * half, 0)
    first = reduce_y(jnp.dot(gram, x2, preferred_element_type=jnp.float32))
    y2 = gather_z(first.astype(jnp.bfloat16))
    second = reduce_y(jnp.dot(gram, y2, preferred_element_type=jnp.float32))
    return (
        coef_a * momentum.astype(jnp.float32) + coef_b * first + coef_c * second
    ).astype(jnp.bfloat16)


def solution(mesh):
    fine = Mesh(mesh.devices.reshape(4, 4, 4, 2, 2), AXES)
    spec = P(("y", "zl"), ("x", "zh", "core"))
    return jax.shard_map(body, mesh=fine, in_specs=(spec,), out_specs=spec, check_vma=False)
```

time: 588 us -> 236 us (0.40)
  the two profiles are of different devices: /device:TPU:1 before, /device:TPU:38 now
where the time goes in v1:
time: 236 us; the launch traced here: 235 us
  waiting for transfers between devices  167 us (71%)
  starting transfers between devices  38.9 us (16%)
  matrix products  11.3 us (5%)
  other arithmetic  9.52 us (4%)
  local copies, waits for them, and re-layouts  7.94 us (3%)
    ppermute x15, waiting for transfers between devices, send_xor(): return lax.ppermute(v, axis, [(i, i ^ k) for i in range(size)])  132 us
    ppermute x9, waiting for transfers between devices, send_up(): return lax.ppermute(v, axis, [(i, (i + k) % size) for i in range(size)])  35.1 us
    ppermute x15, starting transfers between devices, send_xor(): return lax.ppermute(v, axis, [(i, i ^ k) for i in range(size)])  22.8 us
    ppermute x9, starting transfers between devices, send_up(): return lax.ppermute(v, axis, [(i, (i + k) % size) for i in range(size)])  16.1 us
    unnamed x11, local copies, waits for them, and re-layouts  5.44 us
    convert_element_type x1, other arithmetic, body(): chip_sent = chip.astype(jnp.bfloat16)  4.98 us
  transfers between devices with their start and end apart: 24, of which 19 were waited for; matrix products, arithmetic and copies ran while one was open for 1% of the time, Pallas kernels for 0%

profile of v1, /device:TPU:38, one launch (start us, length us, event | category | flops | bytes accessed | tf_op | source)
XLA Modules:
  0.0 235.4 jit_solution(12578615282981121555)
XLA Ops:
  0.1 3.3 %collective-permute-start.4 = (bf16[336,640]{1,0:T(8,128)(2,1)}, bf16[336,640]{1,0:T(8,128)(2,1)S(1)}, u32[]{:S(2)}, u32[]{:S(2)}) collective-permute-start(bf16[336,640]{1,0:T(8,128)(2,1)} %param.1), channel_id=1, source_target_pairs={{0,32},{16,48},{32,0},{48,16},{1,33},{17,49},{33,1},{49,17},{2,34}... | collective-permute-start | bytes 1290248 | tf_op jit(solution)/shard_map/ppermute | solution.py:17
  7.5 10.9 %collective-permute-done.3 = bf16[336,640]{1,0:T(8,128)(2,1)S(1)} collective-permute-done((bf16[336,640]{1,0:T(8,128)(2,1)}, bf16[336,640]{1,0:T(8,128)(2,1)S(1)}, u32[]{:S(2)}, u32[]{:S(2)}) %collective-permute-start.3) | collective-permute-done | bytes 430112 | tf_op jit(solution)/shard_map/ppermute | solution.py:17
  21.1 11.3 %collective-permute-done.4 = bf16[336,640]{1,0:T(8,128)(2,1)S(1)} collective-permute-done((bf16[336,640]{1,0:T(8,128)(2,1)}, bf16[336,640]{1,0:T(8,128)(2,1)S(1)}, u32[]{:S(2)}, u32[]{:S(2)}) %collective-permute-start.4) | collective-permute-done | bytes 430112 | tf_op jit(solution)/shard_map/ppermute | solution.py:17
  32.5 8.9 %collective-permute-done.5 = bf16[336,640]{1,0:T(8,128)(2,1)S(1)} collective-permute-done((bf16[336,640]{1,0:T(8,128)(2,1)}, bf16[336,640]{1,0:T(8,128)(2,1)S(1)}, u32[]{:S(2)}, u32[]{:S(2)}) %collective-permute-start.5) | collective-permute-done | bytes 430112 | tf_op jit(solution)/shard_map/ppermute | solution.py:17
  42.7 4.6 %fusion = f32[1344,1344]{1,0:T(8,128)S(1)} fusion(bf16[1344,640]{1,0:T(8,128)(2,1)S(1)} %constant_dynamic-update-slice_fusion, bf16[336,640]{1,0:T(8,128)(2,1)} %collective-permute-done.2, bf16[336,640]{1,0:T(8,128)(2,1)} %collective-permute-done.1, bf16[336,640]{1,0:T(8,128)(2,1)} %collective-permute-done, bf16[336,640]{1,0:T(8,128)(2,1)S(1)} %copy-done.1), kind=kOutput, calls=%fused_computation.2 | convolution fusion | flops 2318991360 | bytes 10665984 | tf_op jit(solution)/shard_map/dot_general | solution.py:46
  50.7 4.0 %collective-permute-done.6 = bf16[672,1344]{1,0:T(8,128)(2,1)} collective-permute-done((bf16[672,1344]{1,0:T(8,128)(2,1)S(1)}, bf16[672,1344]{1,0:T(8,128)(2,1)}, u32[]{:S(2)}, u32[]{:S(2)}) %collective-permute-start.6) | collective-permute-done | bytes 1806368 | tf_op jit(solution)/shard_map/ppermute | solution.py:17
  54.7 5.0 %fusion.27 = (bf16[672,1344]{1,0:T(8,128)(2,1)S(1)}, f32[672,1344]{1,0:T(8,128)}) fusion(bf16[672,1344]{1,0:T(8,128)(2,1)} %collective-permute-done.6, f32[1344,1344]{1,0:T(8,128)} %copy-done, s32[]{:T(128)S(6)} %select_n.24), kind=kLoop, calls=%fused_computation.46 | loop fusion | flops 2709504 | bytes 10838020 | tf_op jit(solution)/shard_map/convert_element_type | solution.py:53
  65.3 9.2 %collective-permute-done.7 = bf16[168,1344]{1,0:T(8,128)(2,1)S(1)} collective-permute-done((bf16[168,1344]{1,0:T(8,128)(2,1)}, bf16[168,1344]{1,0:T(8,128)(2,1)S(1)}, u32[]{:S(2)}, u32[]{:S(2)}) %collective-permute-start.7) | collective-permute-done | bytes 451616 | tf_op jit(solution)/shard_map/ppermute | solution.py:17
  74.5 9.3 %collective-permute-done.8 = bf16[168,1344]{1,0:T(8,128)(2,1)S(1)} collective-permute-done((bf16[168,1344]{1,0:T(8,128)(2,1)S(1)}, bf16[168,1344]{1,0:T(8,128)(2,1)S(1)}, u32[]{:S(2)}, u32[]{:S(2)}) %collective-permute-start.8) | collective-permute-done | bytes 451616 | tf_op jit(solution)/shard_map/ppermute | solution.py:17
  87.6 5.7 %collective-permute-start.10 = (bf16[168,1344]{1,0:T(8,128)(2,1)S(1)}, bf16[168,1344]{1,0:T(8,128)(2,1)S(1)}, u32[]{:S(2)}, u32[]{:S(2)}) collective-permute-start(bf16[168,1344]{1,0:T(8,128)(2,1)S(1)} %fusion.23), channel_id=1, source_target_pairs={{0,2},{2,0},{1,3},{3,1},{4,6},{6,4},{5,7},{7,5},{8,10},{10,8},{9,1... | collective-permute-start | bytes 1354760 | tf_op jit(solution)/shard_map/ppermute | solution.py:17
  93.3 13.7 %collective-permute-done.10 = bf16[168,1344]{1,0:T(8,128)(2,1)S(1)} collective-permute-done((bf16[168,1344]{1,0:T(8,128)(2,1)S(1)}, bf16[168,1344]{1,0:T(8,128)(2,1)S(1)}, u32[]{:S(2)}, u32[]{:S(2)}) %collective-permute-start.10) | collective-permute-done | bytes 451616 | tf_op jit(solution)/shard_map/ppermute | solution.py:17
  108.8 4.2 %collective-permute-start.12 = (bf16[168,1344]{1,0:T(8,128)(2,1)S(1)}, bf16[168,1344]{1,0:T(8,128)(2,1)S(1)}, u32[]{:S(2)}, u32[]{:S(2)}) collective-permute-start(bf16[168,1344]{1,0:T(8,128)(2,1)S(1)} %get-tuple-element.6), channel_id=1, source_target_pairs={{0,8},{4,12},{8,0},{12,4},{1,9},{5,13},{9,1},{13,5},{2,10},{6,14},... | collective-permute-start | bytes 1354760 | tf_op jit(solution)/shard_map/ppermute | solution.py:17
  113.5 9.0 %collective-permute-done.11 = bf16[168,1344]{1,0:T(8,128)(2,1)S(1)} collective-permute-done((bf16[168,1344]{1,0:T(8,128)(2,1)S(1)}, bf16[168,1344]{1,0:T(8,128)(2,1)S(1)}, u32[]{:S(2)}, u32[]{:S(2)}) %collective-permute-start.11) | collective-permute-done | bytes 451616 | tf_op jit(solution)/shard_map/ppermute | solution.py:17
  122.5 11.4 %collective-permute-done.12 = bf16[168,1344]{1,0:T(8,128)(2,1)S(1)} collective-permute-done((bf16[168,1344]{1,0:T(8,128)(2,1)S(1)}, bf16[168,1344]{1,0:T(8,128)(2,1)S(1)}, u32[]{:S(2)}, u32[]{:S(2)}) %collective-permute-start.12) | collective-permute-done | bytes 451616 | tf_op jit(solution)/shard_map/ppermute | solution.py:17
  137.3 3.3 %collective-permute-done.14 = bf16[672,1344]{1,0:T(8,128)(2,1)S(1)} collective-permute-done((bf16[672,1344]{1,0:T(8,128)(2,1)S(1)}, bf16[672,1344]{1,0:T(8,128)(2,1)S(1)}, u32[]{:S(2)}, u32[]{:S(2)}) %collective-permute-start.14) | collective-permute-done | bytes 1806368 | tf_op jit(solution)/shard_map/ppermute | solution.py:17
  140.8 3.4 %fusion.30 = (bf16[1344,640]{1,0:T(8,128)(2,1)S(1)}, f32[1344,640]{1,0:T(8,128)S(1)}) fusion(bf16[1344,1344]{1,0:T(8,128)(2,1)S(1)} %constant_dynamic-update-slice_fusion.4, bf16[1344,640]{1,0:T(8,128)(2,1)S(1)} %copy-done.3), kind=kOutput, calls=%fused_computation.49 | convolution fusion | flops 2312970240 | bytes 10493952 | tf_op jit(solution)/shard_map/dot_general | solution.py:70
  150.2 7.4 %collective-permute-done.15 = bf16[336,640]{1,0:T(8,128)(2,1)S(1)} collective-permute-done((bf16[336,640]{1,0:T(8,128)(2,1)S(1)}, bf16[336,640]{1,0:T(8,128)(2,1)S(1)}, u32[]{:S(2)}, u32[]{:S(2)}) %collective-permute-start.15) | collective-permute-done | bytes 430112 | tf_op jit(solution)/shard_map/ppermute | solution.py:21
  157.6 10.4 %collective-permute-done.16 = bf16[336,640]{1,0:T(8,128)(2,1)S(1)} collective-permute-done((bf16[336,640]{1,0:T(8,128)(2,1)S(1)}, bf16[336,640]{1,0:T(8,128)(2,1)S(1)}, u32[]{:S(2)}, u32[]{:S(2)}) %collective-permute-start.16) | collective-permute-done | bytes 430112 | tf_op jit(solution)/shard_map/ppermute | solution.py:21
  171.8 13.2 %collective-permute-done.18 = bf16[336,640]{1,0:T(8,128)(2,1)S(1)} collective-permute-done((bf16[336,640]{1,0:T(8,128)(2,1)S(1)}, bf16[336,640]{1,0:T(8,128)(2,1)S(1)}, u32[]{:S(2)}, u32[]{:S(2)}) %collective-permute-start.18) | collective-permute-done | bytes 430112 | tf_op jit(solution)/shard_map/ppermute | solution.py:17
  185.0 14.3 %collective-permute-done.19 = bf16[336,640]{1,0:T(8,128)(2,1)S(1)} collective-permute-done((bf16[336,640]{1,0:T(8,128)(2,1)S(1)}, bf16[336,640]{1,0:T(8,128)(2,1)S(1)}, u32[]{:S(2)}, u32[]{:S(2)}) %collective-permute-start.19) | collective-permute-done | bytes 430112 | tf_op jit(solution)/shard_map/ppermute | solution.py:17
  199.4 8.9 %collective-permute-done.20 = bf16[336,640]{1,0:T(8,128)(2,1)S(1)} collective-permute-done((bf16[336,640]{1,0:T(8,128)(2,1)S(1)}, bf16[336,640]{1,0:T(8,128)(2,1)S(1)}, u32[]{:S(2)}, u32[]{:S(2)}) %collective-permute-start.20) | collective-permute-done | bytes 430112 | tf_op jit(solution)/shard_map/ppermute | solution.py:17
  208.3 3.3 %fusion.31 = (bf16[1344,640]{1,0:T(8,128)(2,1)S(1)}, f32[1344,640]{1,0:T(8,128)S(1)}) fusion(bf16[1344,1344]{1,0:T(8,128)(2,1)S(1)} %constant_dynamic-update-slice_fusion.4, bf16[336,640]{1,0:T(8,128)(2,1)S(1)} %collective-permute-done.20, bf16[336,640]{1,0:T(8,128)(2,1)S(1)} %collective-permute-done.19, bf16[336,640]{1,0:T(8,128)(2,1)S(1)} %collective-permute-done.18, ...), kind=kOutput, calls=%fused_computation.50 | convolution fusion | flops 2319851520 | bytes 10493952 | tf_op jit(solution)/shard_map/dot_general | solution.py:72
  216.8 7.9 %collective-permute-done.21 = bf16[336,640]{1,0:T(8,128)(2,1)S(1)} collective-permute-done((bf16[336,640]{1,0:T(8,128)(2,1)S(1)}, bf16[336,640]{1,0:T(8,128)(2,1)S(1)}, u32[]{:S(2)}, u32[]{:S(2)}) %collective-permute-start.21) | collective-permute-done | bytes 430112 | tf_op jit(solution)/shard_map/ppermute | solution.py:21
  224.6 9.4 %collective-permute-done.22 = bf16[336,640]{1,0:T(8,128)(2,1)S(1)} collective-permute-done((bf16[336,640]{1,0:T(8,128)(2,1)S(1)}, bf16[336,640]{1,0:T(8,128)(2,1)S(1)}, u32[]{:S(2)}, u32[]{:S(2)}) %collective-permute-start.22) | collective-permute-done | bytes 430112 | tf_op jit(solution)/shard_map/ppermute | solution.py:21
  (55 shorter events, 43.1 us)
Async XLA Ops:
  0.0 18.4 %collective-permute-start.3 = (bf16[336,640]{1,0:T(8,128)(2,1)}, bf16[336,640]{1,0:T(8,128)(2,1)S(1)}, u32[]{:S(2)}, u32[]{:S(2)}) collective-permute-start(bf16[336,640]{1,0:T(8,128)(2,1)} %param.1), channel_id=1, source_target_pairs={{0,16},{16,0},{32,48},{48,32},{1,17},{17,1},{33,49},{49,33},{2,18}... | collective-permute-start | bytes 1290248 | tf_op jit(solution)/shard_map/ppermute | solution.py:17
  0.1 32.3 %collective-permute-start.4 = (bf16[336,640]{1,0:T(8,128)(2,1)}, bf16[336,640]{1,0:T(8,128)(2,1)S(1)}, u32[]{:S(2)}, u32[]{:S(2)}) collective-permute-start(bf16[336,640]{1,0:T(8,128)(2,1)} %param.1), channel_id=1, source_target_pairs={{0,32},{16,48},{32,0},{48,16},{1,33},{17,49},{33,1},{49,17},{2,34}... | collective-permute-start | bytes 1290248 | tf_op jit(solution)/shard_map/ppermute | solution.py:17
  3.4 38.0 %collective-permute-start.5 = (bf16[336,640]{1,0:T(8,128)(2,1)}, bf16[336,640]{1,0:T(8,128)(2,1)S(1)}, u32[]{:S(2)}, u32[]{:S(2)}) collective-permute-start(bf16[336,640]{1,0:T(8,128)(2,1)} %param.1), channel_id=1, source_target_pairs={{0,48},{16,32},{32,16},{48,0},{1,49},{17,33},{33,17},{49,1},{2,50}... | collective-permute-start | bytes 1290248 | tf_op jit(solution)/shard_map/ppermute | solution.py:17
  3.8 37.6 %collective-permute-start = (bf16[336,640]{1,0:T(8,128)(2,1)}, bf16[336,640]{1,0:T(8,128)(2,1)}, u32[]{:S(2)}, u32[]{:S(2)}) collective-permute-start(bf16[336,640]{1,0:T(8,128)(2,1)} %param.1), channel_id=1, source_target_pairs={{0,192},{64,0},{128,64},{192,128},{1,193},{65,1},{129,65},{193,129... | collective-permute-start | bytes 1290248 | tf_op jit(solution)/shard_map/ppermute | solution.py:21
  6.9 34.6 %collective-permute-start.1 = (bf16[336,640]{1,0:T(8,128)(2,1)}, bf16[336,640]{1,0:T(8,128)(2,1)}, u32[]{:S(2)}, u32[]{:S(2)}) collective-permute-start(bf16[336,640]{1,0:T(8,128)(2,1)} %param.1), channel_id=1, source_target_pairs={{0,128},{64,192},{128,0},{192,64},{1,129},{65,193},{129,1},{193,65... | collective-permute-start | bytes 1290248 | tf_op jit(solution)/shard_map/ppermute | solution.py:21
  18.4 23.1 %collective-permute-start.2 = (bf16[336,640]{1,0:T(8,128)(2,1)}, bf16[336,640]{1,0:T(8,128)(2,1)}, u32[]{:S(2)}, u32[]{:S(2)}) collective-permute-start(bf16[336,640]{1,0:T(8,128)(2,1)} %param.1), channel_id=1, source_target_pairs={{0,64},{64,128},{128,192},{192,0},{1,65},{65,129},{129,193},{193,1... | collective-permute-start | bytes 1290248 | tf_op jit(solution)/shard_map/ppermute | solution.py:21
  50.6 4.1 %collective-permute-start.6 = (bf16[672,1344]{1,0:T(8,128)(2,1)S(1)}, bf16[672,1344]{1,0:T(8,128)(2,1)}, u32[]{:S(2)}, u32[]{:S(2)}) collective-permute-start(bf16[672,1344]{1,0:T(8,128)(2,1)S(1)} %dynamic-slice_convert_fusion), channel_id=1, source_target_pairs={{0,1},{1,0},{2,3},{3,2},{4,5},{5,4},{6,7},{7,6},{8,9},{9,8},{10,11... | collective-permute-start | bytes 5419016 | tf_op jit(solution)/shard_map/ppermute | solution.py:17
  60.6 13.9 %collective-permute-start.7 = (bf16[168,1344]{1,0:T(8,128)(2,1)}, bf16[168,1344]{1,0:T(8,128)(2,1)S(1)}, u32[]{:S(2)}, u32[]{:S(2)}) collective-permute-start(bf16[168,1344]{1,0:T(8,128)(2,1)} %get-tuple-element.9), channel_id=1, source_target_pairs={{0,4},{4,0},{8,12},{12,8},{1,5},{5,1},{9,13},{13,9},{2,6},{6,2},{1... | collective-permute-start | bytes 1354760 | tf_op jit(solution)/shard_map/ppermute | solution.py:17
  61.4 22.4 %collective-permute-start.8 = (bf16[168,1344]{1,0:T(8,128)(2,1)S(1)}, bf16[168,1344]{1,0:T(8,128)(2,1)S(1)}, u32[]{:S(2)}, u32[]{:S(2)}) collective-permute-start(bf16[168,1344]{1,0:T(8,128)(2,1)S(1)} %get-tuple-element.11), channel_id=1, source_target_pairs={{0,8},{4,12},{8,0},{12,4},{1,9},{5,13},{9,1},{13,5},{2,10},{6,14},... | collective-permute-start | bytes 1354760 | tf_op jit(solution)/shard_map/ppermute | solution.py:17
  62.5 23.7 %collective-permute-start.9 = (bf16[168,1344]{1,0:T(8,128)(2,1)S(1)}, bf16[168,1344]{1,0:T(8,128)(2,1)S(1)}, u32[]{:S(2)}, u32[]{:S(2)}) collective-permute-start(bf16[168,1344]{1,0:T(8,128)(2,1)S(1)} %get-tuple-element.10), channel_id=1, source_target_pairs={{0,12},{4,8},{8,4},{12,0},{1,13},{5,9},{9,5},{13,1},{2,14},{6,10},... | collective-permute-start | bytes 1354760 | tf_op jit(solution)/shard_map/ppermute | solution.py:17
  87.6 19.4 %collective-permute-start.10 = (bf16[168,1344]{1,0:T(8,128)(2,1)S(1)}, bf16[168,1344]{1,0:T(8,128)(2,1)S(1)}, u32[]{:S(2)}, u32[]{:S(2)}) collective-permute-start(bf16[168,1344]{1,0:T(8,128)(2,1)S(1)} %fusion.23), channel_id=1, source_target_pairs={{0,2},{2,0},{1,3},{3,1},{4,6},{6,4},{5,7},{7,5},{8,10},{10,8},{9,1... | collective-permute-start | bytes 1354760 | tf_op jit(solution)/shard_map/ppermute | solution.py:17
  108.7 13.8 %collective-permute-start.11 = (bf16[168,1344]{1,0:T(8,128)(2,1)S(1)}, bf16[168,1344]{1,0:T(8,128)(2,1)S(1)}, u32[]{:S(2)}, u32[]{:S(2)}) collective-permute-start(bf16[168,1344]{1,0:T(8,128)(2,1)S(1)} %get-tuple-element.6), channel_id=1, source_target_pairs={{0,4},{4,0},{8,12},{12,8},{1,5},{5,1},{9,13},{13,9},{2,6},{6,2},{1... | collective-permute-start | bytes 1354760 | tf_op jit(solution)/shard_map/ppermute | solution.py:17
  108.8 25.1 %collective-permute-start.12 = (bf16[168,1344]{1,0:T(8,128)(2,1)S(1)}, bf16[168,1344]{1,0:T(8,128)(2,1)S(1)}, u32[]{:S(2)}, u32[]{:S(2)}) collective-permute-start(bf16[168,1344]{1,0:T(8,128)(2,1)S(1)} %get-tuple-element.6), channel_id=1, source_target_pairs={{0,8},{4,12},{8,0},{12,4},{1,9},{5,13},{9,1},{13,5},{2,10},{6,14},... | collective-permute-start | bytes 1354760 | tf_op jit(solution)/shard_map/ppermute | solution.py:17
  113.0 23.5 %collective-permute-start.13 = (bf16[168,1344]{1,0:T(8,128)(2,1)S(1)}, bf16[168,1344]{1,0:T(8,128)(2,1)S(1)}, u32[]{:S(2)}, u32[]{:S(2)}) collective-permute-start(bf16[168,1344]{1,0:T(8,128)(2,1)S(1)} %get-tuple-element.6), channel_id=1, source_target_pairs={{0,12},{4,8},{8,4},{12,0},{1,13},{5,9},{9,5},{13,1},{2,14},{6,10},... | collective-permute-start | bytes 1354760 | tf_op jit(solution)/shard_map/ppermute | solution.py:17
  136.6 4.0 %collective-permute-start.14 = (bf16[672,1344]{1,0:T(8,128)(2,1)S(1)}, bf16[672,1344]{1,0:T(8,128)(2,1)S(1)}, u32[]{:S(2)}, u32[]{:S(2)}) collective-permute-start(bf16[672,1344]{1,0:T(8,128)(2,1)S(1)} %constant_dynamic-update-slice_fusion.6), channel_id=1, source_target_pairs={{0,1},{1,0},{2,3},{3,2},{4,5},{5,4},{6,7},{7,6},{8,9},{9,8},{10,11... | collective-permute-start | bytes 5419016 | tf_op jit(solution)/shard_map/ppermute | solution.py:17
  144.3 13.3 %collective-permute-start.15 = (bf16[336,640]{1,0:T(8,128)(2,1)S(1)}, bf16[336,640]{1,0:T(8,128)(2,1)S(1)}, u32[]{:S(2)}, u32[]{:S(2)}) collective-permute-start(bf16[336,640]{1,0:T(8,128)(2,1)S(1)} %get-tuple-element.15), channel_id=1, source_target_pairs={{0,64},{64,128},{128,192},{192,0},{1,65},{65,129},{129,193},{193,1... | collective-permute-start | bytes 1290248 | tf_op jit(solution)/shard_map/ppermute | solution.py:21
  146.0 22.0 %collective-permute-start.16 = (bf16[336,640]{1,0:T(8,128)(2,1)S(1)}, bf16[336,640]{1,0:T(8,128)(2,1)S(1)}, u32[]{:S(2)}, u32[]{:S(2)}) collective-permute-start(bf16[336,640]{1,0:T(8,128)(2,1)S(1)} %get-tuple-element.17), channel_id=1, source_target_pairs={{0,128},{64,192},{128,0},{192,64},{1,129},{65,193},{129,1},{193,65... | collective-permute-start | bytes 1290248 | tf_op jit(solution)/shard_map/ppermute | solution.py:21
  148.9 19.1 %collective-permute-start.17 = (bf16[336,640]{1,0:T(8,128)(2,1)S(1)}, bf16[336,640]{1,0:T(8,128)(2,1)S(1)}, u32[]{:S(2)}, u32[]{:S(2)}) collective-permute-start(bf16[336,640]{1,0:T(8,128)(2,1)S(1)} %get-tuple-element.16), channel_id=1, source_target_pairs={{0,192},{64,0},{128,64},{192,128},{1,193},{65,1},{129,65},{193,129... | collective-permute-start | bytes 1290248 | tf_op jit(solution)/shard_map/ppermute | solution.py:21
  168.2 16.8 %collective-permute-start.18 = (bf16[336,640]{1,0:T(8,128)(2,1)S(1)}, bf16[336,640]{1,0:T(8,128)(2,1)S(1)}, u32[]{:S(2)}, u32[]{:S(2)}) collective-permute-start(bf16[336,640]{1,0:T(8,128)(2,1)S(1)} %fusion.24), channel_id=1, source_target_pairs={{0,16},{16,0},{32,48},{48,32},{1,17},{17,1},{33,49},{49,33},{2,18}... | collective-permute-start | bytes 1290248 | tf_op jit(solution)/shard_map/ppermute | solution.py:17
  168.3 31.0 %collective-permute-start.19 = (bf16[336,640]{1,0:T(8,128)(2,1)S(1)}, bf16[336,640]{1,0:T(8,128)(2,1)S(1)}, u32[]{:S(2)}, u32[]{:S(2)}) collective-permute-start(bf16[336,640]{1,0:T(8,128)(2,1)S(1)} %fusion.24), channel_id=1, source_target_pairs={{0,32},{16,48},{32,0},{48,16},{1,33},{17,49},{33,1},{49,17},{2,34}... | collective-permute-start | bytes 1290248 | tf_op jit(solution)/shard_map/ppermute | solution.py:17
  170.6 37.7 %collective-permute-start.20 = (bf16[336,640]{1,0:T(8,128)(2,1)S(1)}, bf16[336,640]{1,0:T(8,128)(2,1)S(1)}, u32[]{:S(2)}, u32[]{:S(2)}) collective-permute-start(bf16[336,640]{1,0:T(8,128)(2,1)S(1)} %fusion.24), channel_id=1, source_target_pairs={{0,48},{16,32},{32,16},{48,0},{1,49},{17,33},{33,17},{49,1},{2,50}... | collective-permute-start | bytes 1290248 | tf_op jit(solution)/shard_map/ppermute | solution.py:17
  211.8 12.9 %collective-permute-start.21 = (bf16[336,640]{1,0:T(8,128)(2,1)S(1)}, bf16[336,640]{1,0:T(8,128)(2,1)S(1)}, u32[]{:S(2)}, u32[]{:S(2)}) collective-permute-start(bf16[336,640]{1,0:T(8,128)(2,1)S(1)} %get-tuple-element.12), channel_id=1, source_target_pairs={{0,64},{64,128},{128,192},{192,0},{1,65},{65,129},{129,193},{193,1... | collective-permute-start | bytes 1290248 | tf_op jit(solution)/shard_map/ppermute | solution.py:21
  213.1 21.0 %collective-permute-start.22 = (bf16[336,640]{1,0:T(8,128)(2,1)S(1)}, bf16[336,640]{1,0:T(8,128)(2,1)S(1)}, u32[]{:S(2)}, u32[]{:S(2)}) collective-permute-start(bf16[336,640]{1,0:T(8,128)(2,1)S(1)} %get-tuple-element.14), channel_id=1, source_target_pairs={{0,128},{64,192},{128,0},{192,64},{1,129},{65,193},{129,1},{193,65... | collective-permute-start | bytes 1290248 | tf_op jit(solution)/shard_map/ppermute | solution.py:21
  216.2 17.9 %collective-permute-start.23 = (bf16[336,640]{1,0:T(8,128)(2,1)S(1)}, bf16[336,640]{1,0:T(8,128)(2,1)S(1)}, u32[]{:S(2)}, u32[]{:S(2)}) collective-permute-start(bf16[336,640]{1,0:T(8,128)(2,1)S(1)} %get-tuple-element.13), channel_id=1, source_target_pairs={{0,192},{64,0},{128,64},{192,128},{1,193},{65,1},{129,65},{193,129... | collective-permute-start | bytes 1290248 | tf_op jit(solution)/shard_map/ppermute | solution.py:21
  (4 other events, 50.5 us)
